TPU v7x, 32 devices: a whole 2x2x4 slice. The times are simulated.
32 devices in a mesh: outer: 8 (over z, y), inner: 4 (over x, core).
Axes of the slice: x: 2, y: 2, z: 4, core: 2. Of those that a mesh axis runs over, the one named last changes fastest.
Arguments:
- stem_real: float32 [8, 4, 256, 512], P('outer', 'inner'), may hold values from -6 to 6
- stem_imag: float32 [8, 4, 256, 512], P('outer', 'inner'), may hold values from -6 to 6
- branch_real: float32 [4, 512, 512], replicated, may hold values from -0.1875 to 0.1875
- branch_imag: float32 [4, 512, 512], replicated, may hold values from -0.1875 to 0.1875
- orders: int32 [4, 512], replicated, may hold values from 0 to 511, each once within a row
Outputs:
- out_real: float32 [8, 4, 256, 512], P('outer', 'inner')
- out_imag: float32 [8, 4, 256, 512], P('outer', 'inner')
Inputs may be any that keep to these rules, and one draw needn't show every extreme that they name: Each row of orders holds every index of 0 to 511 once.
All inputs are finite; a program needn't handle non-finite values.
Results may differ from a plain program's by a relative error of at most 0.0001.
Values sent between devices are 32-bit elements; how exact they have to be, the bound alone decides.
A program may use at most 64 MiB of HBM per device.

v0:
```python
import jax
import jax.numpy as jnp
from jax import lax
from jax.sharding import PartitionSpec as P

PRODUCTS = 4


def partner(x, axis, stride):
    return lax.ppermute(x, axis, [(i, i ^ 1 << stride) for i in range(lax.axis_size(axis))])


def prepare(branch_real, branch_imag, order):
    width = branch_real.shape[0]
    places = lax.broadcasted_iota(jnp.int32, (width, width), 0)
    selector = (places == order[None, :]).astype(jnp.float32)
    moved_real = jnp.dot(
        selector, branch_real, precision=lax.Precision.HIGHEST, preferred_element_type=jnp.float32
    )
    moved_imag = jnp.dot(
        selector, branch_imag, precision=lax.Precision.HIGHEST, preferred_element_type=jnp.float32
    )
    return (moved_real, moved_imag, moved_real + moved_imag)


def product(plane_real, plane_imag, prepared):
    moved_real, moved_imag, moved_sum = prepared
    width = moved_real.shape[0]
    count = plane_real.size // width
    left_real = plane_real.reshape(count, width)
    left_imag = plane_imag.reshape(count, width)
    first = jnp.dot(
        left_real, moved_real, precision=lax.Precision.HIGHEST, preferred_element_type=jnp.float32
    )
    second = jnp.dot(
        left_imag, moved_imag, precision=lax.Precision.HIGHEST, preferred_element_type=jnp.float32
    )
    third = jnp.dot(
        left_real + left_imag,
        moved_sum,
        precision=lax.Precision.HIGHEST,
        preferred_element_type=jnp.float32,
    )
    return (
        (first - second).reshape(1, 1, count, width),
        (third - first - second).reshape(1, 1, count, width),
    )


def pair_section(plane, groups, section, own_bit):
    rows_n, width = (plane.shape[2], plane.shape[3])
    upper = groups >> section + 1
    lower = 1 << section
    viewed = plane.reshape(rows_n, upper, 2, lower * (width // groups))
    half_zero = viewed[:, :, 0]
    half_one = viewed[:, :, 1]
    keeps_one = own_bit == 1
    outgoing = jnp.where(keeps_one, half_zero, half_one)
    return (half_zero, half_one, outgoing, keeps_one)


def settle(plane, half_zero, half_one, received, keeps_one):
    new_zero = jnp.where(keeps_one, received, half_zero)
    new_one = jnp.where(keeps_one, half_one, received)
    return jnp.stack([new_zero, new_one], axis=2).reshape(plane.shape)


def paired_swap(plane_real, plane_imag, groups, device, exchanger):
    for section in range(groups.bit_length() - 1):
        own_bit = device >> section & 1
        zero_real, one_real, out_real, keeps_one = pair_section(
            plane_real, groups, section, own_bit
        )
        zero_imag, one_imag, out_imag, keeps_one = pair_section(
            plane_imag, groups, section, own_bit
        )
        recv_real, recv_imag = exchanger((out_real, out_imag), section)
        plane_real = settle(plane_real, zero_real, one_real, recv_real, keeps_one)
        plane_imag = settle(plane_imag, zero_imag, one_imag, recv_imag, keeps_one)
    return (plane_real, plane_imag)


def inner_step(plane_real, plane_imag, prepared):
    groups = lax.axis_size("inner")

    def exchanger(pieces, section):
        return partner(pieces, "inner", section)

    plane_real, plane_imag = paired_swap(
        plane_real, plane_imag, groups, lax.axis_index("inner"), exchanger
    )
    return product(plane_real, plane_imag, prepared)


def outer_step(plane_real, plane_imag, prepared):
    return product(
        lax.all_to_all(plane_real, "outer", split_axis=3, concat_axis=3, tiled=True),
        lax.all_to_all(plane_imag, "outer", split_axis=3, concat_axis=3, tiled=True),
        prepared,
    )


def on_device(stem_real, stem_imag, branch_real, branch_imag, orders):
    tables = [
        prepare(branch_real[step], branch_imag[step], orders[step]) for step in range(PRODUCTS)
    ]
    plane_real, plane_imag = product(stem_real, stem_imag, tables[0])
    plane_real, plane_imag = inner_step(plane_real, plane_imag, tables[1])
    plane_real, plane_imag = outer_step(plane_real, plane_imag, tables[2])
    plane_real, plane_imag = inner_step(plane_real, plane_imag, tables[3])
    return (plane_real, plane_imag)


def solution(mesh):
    placed = (P("outer", "inner", None, None), P("outer", "inner", None, None), P(), P(), P())
    return jax.shard_map(
        on_device,
        mesh=mesh,
        in_specs=placed,
        out_specs=(P("outer", "inner", None, None), P("outer", "inner", None, None)),
        check_vma=False,
    )
```

profile of v0, /device:TPU:0, one launch (start us, length us, event | category | flops | bytes accessed | tf_op | source)
XLA Modules:
  0.0 109.3 jit_solution(4318021733966090813)
XLA Ops:
  0.6 0.9 fusion.68
  1.5 2.3 %fusion.18 = f32[512,512]{1,0:T(8,128)S(1)} fusion(f32[4,512,512]{2,1,0:T(8,128)} %param.8, s32[512]{0:T(512)S(1)} %bitcast.250), kind=kOutput, calls=%fused_computation.24 | convolution fusion | flops 1610874880 | bytes 2099200 | tf_op jit(solution)/shard_map/dot_general | solution.py:20
  3.8 2.3 %fusion.20 = f32[512,512]{1,0:T(8,128)S(1)} fusion(f32[4,512,512]{2,1,0:T(8,128)} %param.7, s32[512]{0:T(512)S(1)} %bitcast.251), kind=kOutput, calls=%fused_computation.26 | convolution fusion | flops 1610874880 | bytes 2099200 | tf_op jit(solution)/shard_map/dot_general | solution.py:17
  6.2 1.8 %convolution_bitcast_fusion = f32[256,512]{0,1:T(8,128)S(1)} fusion(f32[512,512]{1,0:T(8,128)S(1)} %fusion.18, f32[1,1,256,512]{3,2,1,0:T(8,128)S(1)} %copy-done.1), kind=kOutput, calls=%fused_computation.10 | convolution fusion | flops 805306368 | bytes 2097152 | tf_op jit(solution)/shard_map/dot_general | solution.py:35
  8.0 2.9 %fusion.69 = (f32[256,512]{0,1:T(8,128)S(1)}, f32[256,512]{0,1:T(8,128)S(1)}) fusion(f32[256,512]{0,1:T(8,128)S(1)} %convolution_bitcast_fusion, f32[512,512]{1,0:T(8,128)S(1)} %fusion.20, f32[1,1,256,512]{3,2,1,0:T(8,128)} %param.5), kind=kOutput, calls=%fused_computation.121 | convolution fusion | flops 805437440 | bytes 3145728 | tf_op jit(solution)/shard_map/dot_general | solution.py:32
  10.8 0.7 fusion.60
  11.6 0.5 collective-permute-start
  12.0 3.0 %fusion = f32[256,512]{0,1:T(8,128)S(1)} fusion(f32[256,512]{0,1:T(8,128)S(1)} %convolution_bitcast_fusion, f32[256,512]{0,1:T(8,128)S(1)} %get-tuple-element.27, f32[512,512]{1,0:T(8,128)S(1)} %fusion.20, f32[512,512]{1,0:T(8,128)S(1)} %fusion.18, f32[1,1,256,512]{3,2,1,0:T(8,128)} %param.6, f32[1,1,256,512]{3,2,1,0:T(8,128)} %param.5), kind=kOutput, calls=%fused_computation.4 | convolution fusion | flops 805961728 | bytes 4718592 | tf_op jit(solution)/shard_map/dot_general | solution.py:38
  15.2 2.3 %fusion.16 = f32[512,512]{1,0:T(8,128)S(1)} fusion(f32[4,512,512]{2,1,0:T(8,128)} %param.7, s32[512]{0:T(512)S(1)} %bitcast.248), kind=kOutput, calls=%fused_computation.22 | convolution fusion | flops 1610874880 | bytes 2099200 | tf_op jit(solution)/shard_map/dot_general | solution.py:17
  17.5 2.3 %fusion.14 = f32[512,512]{1,0:T(8,128)S(1)} fusion(f32[4,512,512]{2,1,0:T(8,128)} %param.8, s32[512]{0:T(512)S(1)} %bitcast.249), kind=kOutput, calls=%fused_computation.20 | convolution fusion | flops 1610874880 | bytes 2099200 | tf_op jit(solution)/shard_map/dot_general | solution.py:20
  20.0 3.0 %collective-permute-start.1 = (f32[256,1,256]{0,2,1:T(8,128)S(1)}, f32[256,1,256]{0,2,1:T(8,128)S(1)}, u32[]{:S(2)}, u32[]{:S(2)}) collective-permute-start(f32[256,1,256]{0,2,1:T(8,128)S(1)} %fusion.61), channel_id=1, source_target_pairs={{0,2},{1,3},{2,0},{3,1},{4,6},{5,7},{6,4},{7,5},{8,10},{9,11},{10,... | collective-permute-start | bytes 786440 | tf_op jit(solution)/shard_map/ppermute | solution.py:10
  23.3 6.8 %collective-permute-done.1 = f32[256,1,256]{0,2,1:T(8,128)S(1)} collective-permute-done((f32[256,1,256]{0,2,1:T(8,128)S(1)}, f32[256,1,256]{0,2,1:T(8,128)S(1)}, u32[]{:S(2)}, u32[]{:S(2)}) %collective-permute-start.1) | collective-permute-done | bytes 262176 | tf_op jit(solution)/shard_map/ppermute | solution.py:10
  30.2 1.1 fusion.71
  31.3 3.8 %collective-permute-done.3 = f32[256,1,256]{0,2,1:T(8,128)S(1)} collective-permute-done((f32[256,1,256]{0,2,1:T(8,128)S(1)}, f32[256,1,256]{0,2,1:T(8,128)S(1)}, u32[]{:S(2)}, u32[]{:S(2)}) %collective-permute-start.3) | collective-permute-done | bytes 262176 | tf_op jit(solution)/shard_map/ppermute | solution.py:10
  35.2 1.3 %fusion.72 = f32[256,512]{1,0:T(8,128)S(1)} fusion(f32[256,512]{0,1:T(8,128)S(1)} %bitcast.240, f32[512,512]{1,0:T(8,128)S(1)} %fusion.14), kind=kOutput, calls=%fused_computation.124 | convolution fusion | flops 805306368 | bytes 2097152 | tf_op jit(solution)/shard_map/dot_general | solution.py:35
  36.5 1.1 %fusion.2 = f32[1,1,256,512]{3,2,1,0:T(8,128)S(1)} fusion(f32[256,512]{1,0:T(8,128)S(1)} %fusion.72, f32[256,512]{1,0:T(8,128)S(1)} %fusion.71, f32[512,512]{1,0:T(8,128)S(1)} %fusion.16, f32[512,512]{1,0:T(8,128)S(1)} %fusion.14, f32[256,512]{0,1:T(8,128)S(1)} %bitcast.239, f32[256,512]{0,1:T(8,128)S(1)} %bitcast.241), kind=kOutput, calls=%fused_computation.6 | convolution fusion | flops 805961728 | bytes 4718592 | tf_op jit(solution)/shard_map/dot_general | solution.py:38
  37.6 1.0 copy.36
  38.7 6.1 %all-to-all-start.1 = ((f32[1,1,256,512]{2,1,0,3:T(1,128)}), f32[1,1,256,512]{2,1,0,3:T(1,128)S(1)}, u32[]{:S(2)}, u32[]{:S(2)}) async-start(f32[1,1,256,512]{2,1,0,3:T(1,128)} %copy.36), calls=%async_computation.1 | async-start | bytes 1048576 | tf_op jit(solution)/shard_map/all_to_all | solution.py:98
  44.7 3.3 %fusion.10 = f32[512,512]{1,0:T(8,128)} fusion(f32[4,512,512]{2,1,0:T(8,128)} %param.8, s32[512]{0:T(512)S(1)} %bitcast.246), kind=kOutput, calls=%fused_computation.16 | convolution fusion | flops 1610874880 | bytes 2099200 | tf_op jit(solution)/shard_map/dot_general | solution.py:20
  48.1 1.0 copy.35
  49.2 9.4 %all-to-all-done.1 = f32[1,1,256,512]{2,1,0,3:T(1,128)S(1)} async-done(((f32[1,1,256,512]{2,1,0,3:T(1,128)}), f32[1,1,256,512]{2,1,0,3:T(1,128)S(1)}, u32[]{:S(2)}, u32[]{:S(2)}) %all-to-all-start.1) | async-done | bytes 524320 | tf_op jit(solution)/shard_map/all_to_all | solution.py:98
  58.6 4.2 %all-to-all-start = ((f32[1,1,256,512]{2,1,0,3:T(1,128)}), f32[1,1,256,512]{2,1,0,3:T(1,128)}, u32[]{:S(2)}, u32[]{:S(2)}) async-start(f32[1,1,256,512]{2,1,0,3:T(1,128)} %copy.35), calls=%async_computation | async-start | bytes 1048576 | tf_op jit(solution)/shard_map/all_to_all | solution.py:97
  62.8 2.3 %fusion.12 = f32[512,512]{1,0:T(8,128)S(1)} fusion(f32[4,512,512]{2,1,0:T(8,128)} %param.7, s32[512]{0:T(512)S(1)} %bitcast.247), kind=kOutput, calls=%fused_computation.18 | convolution fusion | flops 1610874880 | bytes 2099200 | tf_op jit(solution)/shard_map/dot_general | solution.py:17
  65.1 2.3 %fusion.6 = f32[512,512]{1,0:T(8,128)S(1)} fusion(f32[4,512,512]{2,1,0:T(8,128)} %param.8, s32[512]{0:T(512)S(1)} %bitcast.244), kind=kOutput, calls=%fused_computation.12 | convolution fusion | flops 1610874880 | bytes 2099200 | tf_op jit(solution)/shard_map/dot_general | solution.py:20
  67.4 2.3 %fusion.8 = f32[512,512]{1,0:T(8,128)S(1)} fusion(f32[4,512,512]{2,1,0:T(8,128)} %param.7, s32[512]{0:T(512)S(1)} %bitcast.245), kind=kOutput, calls=%fused_computation.14 | convolution fusion | flops 1610874880 | bytes 2099200 | tf_op jit(solution)/shard_map/dot_general | solution.py:17
  69.7 3.2 %fusion.34 = f32[256,512]{1,0:T(8,128)} fusion(f32[512,512]{1,0:T(8,128)} %fusion.10, f32[1,1,256,512]{2,1,0,3:T(1,128)} %copy-done), kind=kOutput, calls=%fused_computation.53 | convolution fusion | flops 805306368 | bytes 2097152 | tf_op jit(solution)/shard_map/dot_general | solution.py:35
  73.0 3.5 %all-to-all-done = f32[1,1,256,512]{2,1,0,3:T(1,128)} async-done(((f32[1,1,256,512]{2,1,0,3:T(1,128)}), f32[1,1,256,512]{2,1,0,3:T(1,128)}, u32[]{:S(2)}, u32[]{:S(2)}) %all-to-all-start) | async-done | bytes 524320 | tf_op jit(solution)/shard_map/all_to_all | solution.py:97
  76.5 3.1 %fusion.70 = (f32[256,512]{1,0:T(8,128)}, f32[256,512]{1,0:T(8,128)S(1)}) fusion(f32[256,512]{1,0:T(8,128)} %fusion.34, f32[512,512]{1,0:T(8,128)S(1)} %fusion.12, f32[1,1,256,512]{2,1,0,3:T(1,128)} %all-to-all-done), kind=kOutput, calls=%fused_computation.122 | convolution fusion | flops 805437440 | bytes 3145728 | tf_op jit(solution)/shard_map/dot_general | solution.py:32
  79.5 3.6 %fusion.3 = f32[256,512]{1,0:T(8,128)} fusion(f32[256,512]{1,0:T(8,128)} %fusion.34, f32[256,512]{1,0:T(8,128)S(1)} %get-tuple-element.29, f32[512,512]{1,0:T(8,128)S(1)} %fusion.12, f32[512,512]{1,0:T(8,128)} %fusion.10, f32[1,1,256,512]{2,1,0,3:T(1,128)} %copy-done, f32[1,1,256,512]{2,1,0,3:T(1,128)} %all-to-all-done), kind=kOutput, calls=%fused_computation.7 | convolution fusion | flops 805961728 | bytes 4718592 | tf_op jit(solution)/shard_map/dot_general | solution.py:38
  83.1 1.4 %reshape_reshape.45 = f32[256,2,2,128]{3,2,1,0:T(2,128)S(1)} reshape(f32[256,512]{1,0:T(8,128)} %fusion.3) | data formatting | bytes 1048576 | tf_op jit(solution)/shard_map/reshape;reshape | solution.py:54
  84.5 0.4 fusion.66
  84.9 0.1 copy.52
  85.0 0.1 copy.53
  85.2 0.7 bitcast_select_fusion.1
  85.9 1.4 %reshape_reshape.42 = f32[256,2,2,128]{3,2,1,0:T(2,128)S(1)} reshape(f32[256,512]{1,0:T(8,128)} %get-tuple-element.28) | data formatting | bytes 1048576 | tf_op jit(solution)/shard_map/reshape;reshape | solution.py:54
  87.3 1.1 %fusion.67 = (f32[256,2,1,128]{3,2,1,0:T(1,128)}, f32[256,2,1,128]{3,2,1,0:T(1,128)S(1)}) fusion(f32[256,2,2,128]{3,2,1,0:T(2,128)S(1)} %reshape_reshape.42), kind=kLoop, calls=%fused_computation.119 | loop fusion | bytes 1048576 | tf_op jit(solution)/shard_map/slice | solution.py:55
  88.4 1.1 copy.50
  89.5 0.1 copy.51
  89.7 0.6 collective-permute-start.4
  90.3 1.0 fusion.57
  91.4 1.6 %collective-permute-start.7 = (f32[256,1,256]{0,2,1:T(8,128)S(1)}, f32[256,1,256]{0,2,1:T(8,128)S(1)}, u32[]{:S(2)}, u32[]{:S(2)}) collective-permute-start(f32[256,1,256]{0,2,1:T(8,128)S(1)} %fusion.65), channel_id=1, source_target_pairs={{0,2},{1,3},{2,0},{3,1},{4,6},{5,7},{6,4},{7,5},{8,10},{9,11},{10,... | collective-permute-start | bytes 786440 | tf_op jit(solution)/shard_map/ppermute | solution.py:10
  93.1 0.6 collective-permute-start.5
  93.7 6.9 %collective-permute-done.7 = f32[256,1,256]{0,2,1:T(8,128)S(1)} collective-permute-done((f32[256,1,256]{0,2,1:T(8,128)S(1)}, f32[256,1,256]{0,2,1:T(8,128)S(1)}, u32[]{:S(2)}, u32[]{:S(2)}) %collective-permute-start.7) | collective-permute-done | bytes 262176 | tf_op jit(solution)/shard_map/ppermute | solution.py:10
  100.7 1.1 fusion.74
  101.8 3.5 %collective-permute-done.5 = f32[256,1,256]{0,2,1:T(8,128)S(1)} collective-permute-done((f32[256,1,256]{0,2,1:T(8,128)S(1)}, f32[256,1,256]{0,2,1:T(8,128)S(1)}, u32[]{:S(2)}, u32[]{:S(2)}) %collective-permute-start.5) | collective-permute-done | bytes 262176 | tf_op jit(solution)/shard_map/ppermute | solution.py:10
  105.4 1.1 fusion.73
  106.5 1.9 %fusion.5 = f32[1,1,256,512]{3,2,1,0:T(8,128)} fusion(f32[256,512]{1,0:T(8,128)S(1)} %fusion.74, f32[256,512]{1,0:T(8,128)S(1)} %fusion.73, f32[512,512]{1,0:T(8,128)S(1)} %fusion.8, f32[512,512]{1,0:T(8,128)S(1)} %fusion.6, f32[256,512]{0,1:T(8,128)S(1)} %bitcast.243, f32[256,512]{0,1:T(8,128)S(1)} %bitcast.237), kind=kOutput, calls=%fused_computation.9 | convolution fusion | flops 805961728 | bytes 4718592 | tf_op jit(solution)/shard_map/dot_general | solution.py:38
  108.4 0.9 subtract_bitcast_fusion
  (36 shorter events, 1.3 us)
Async XLA Ops:
  0.6 5.5 %copy-start.1 = (f32[1,1,256,512]{3,2,1,0:T(8,128)S(1)}, f32[1,1,256,512]{3,2,1,0:T(8,128)}, u32[]{:S(2)}) copy-start(f32[1,1,256,512]{3,2,1,0:T(8,128)} %param.6) | copy-start | bytes 1572868
  11.6 8.3 %collective-permute-start = (f32[256,2,128]{0,2,1:T(8,128)}, f32[256,2,128]{0,2,1:T(8,128)S(1)}, u32[]{:S(2)}, u32[]{:S(2)}) collective-permute-start(f32[256,2,128]{0,2,1:T(8,128)} %fusion.60), channel_id=1, source_target_pairs={{0,1},{1,0},{2,3},{3,2},{4,5},{5,4},{6,7},{7,6},{8,9},{9,8},{10,11... | collective-permute-start | bytes 786440 | tf_op jit(solution)/shard_map/ppermute | solution.py:10
  15.1 7.9 %collective-permute-start.2 = (f32[256,2,128]{0,2,1:T(8,128)S(1)}, f32[256,2,128]{0,2,1:T(8,128)S(1)}, u32[]{:S(2)}, u32[]{:S(2)}) collective-permute-start(f32[256,2,128]{0,2,1:T(8,128)S(1)} %fusion.62), channel_id=1, source_target_pairs={{0,1},{1,0},{2,3},{3,2},{4,5},{5,4},{6,7},{7,6},{8,9},{9,8},{10,11... | collective-permute-start | bytes 786440 | tf_op jit(solution)/shard_map/ppermute | solution.py:10
  20.0 10.1 %collective-permute-start.1 = (f32[256,1,256]{0,2,1:T(8,128)S(1)}, f32[256,1,256]{0,2,1:T(8,128)S(1)}, u32[]{:S(2)}, u32[]{:S(2)}) collective-permute-start(f32[256,1,256]{0,2,1:T(8,128)S(1)} %fusion.61), channel_id=1, source_target_pairs={{0,2},{1,3},{2,0},{3,1},{4,6},{5,7},{6,4},{7,5},{8,10},{9,11},{10,... | collective-permute-start | bytes 786440 | tf_op jit(solution)/shard_map/ppermute | solution.py:10
  23.2 11.9 %collective-permute-start.3 = (f32[256,1,256]{0,2,1:T(8,128)S(1)}, f32[256,1,256]{0,2,1:T(8,128)S(1)}, u32[]{:S(2)}, u32[]{:S(2)}) collective-permute-start(f32[256,1,256]{0,2,1:T(8,128)S(1)} %fusion.63), channel_id=1, source_target_pairs={{0,2},{1,3},{2,0},{3,1},{4,6},{5,7},{6,4},{7,5},{8,10},{9,11},{10,... | collective-permute-start | bytes 786440 | tf_op jit(solution)/shard_map/ppermute | solution.py:10
  38.7 20.0 %all-to-all-start.1 = ((f32[1,1,256,512]{2,1,0,3:T(1,128)}), f32[1,1,256,512]{2,1,0,3:T(1,128)S(1)}, u32[]{:S(2)}, u32[]{:S(2)}) async-start(f32[1,1,256,512]{2,1,0,3:T(1,128)} %copy.36), calls=%async_computation.1 | async-start | bytes 1048576 | tf_op jit(solution)/shard_map/all_to_all | solution.py:98
  58.6 6.5 %copy-start = (f32[1,1,256,512]{2,1,0,3:T(1,128)}, f32[1,1,256,512]{2,1,0,3:T(1,128)S(1)}, u32[]{:S(2)}) copy-start(f32[1,1,256,512]{2,1,0,3:T(1,128)S(1)} %all-to-all-done.1) | copy-start | bytes 1572868
  58.6 17.9 %all-to-all-start = ((f32[1,1,256,512]{2,1,0,3:T(1,128)}), f32[1,1,256,512]{2,1,0,3:T(1,128)}, u32[]{:S(2)}, u32[]{:S(2)}) async-start(f32[1,1,256,512]{2,1,0,3:T(1,128)} %copy.35), calls=%async_computation | async-start | bytes 1048576 | tf_op jit(solution)/shard_map/all_to_all | solution.py:97
  85.9 4.3 %collective-permute-start.6 = (f32[256,2,128]{0,2,1:T(8,128)}, f32[256,2,128]{0,2,1:T(8,128)}, u32[]{:S(2)}, u32[]{:S(2)}) collective-permute-start(f32[256,2,128]{0,2,1:T(8,128)} %bitcast_select_fusion.1), channel_id=1, source_target_pairs={{0,1},{1,0},{2,3},{3,2},{4,5},{5,4},{6,7},{7,6},{8,9},{9,8},{10,11... | collective-permute-start | bytes 786440 | tf_op jit(solution)/shard_map/ppermute | solution.py:10
  89.7 3.3 %collective-permute-start.4 = (f32[256,2,128]{0,2,1:T(8,128)S(1)}, f32[256,2,128]{0,2,1:T(8,128)S(1)}, u32[]{:S(2)}, u32[]{:S(2)}) collective-permute-start(f32[256,2,128]{0,2,1:T(8,128)S(1)} %bitcast_select_fusion.4), channel_id=1, source_target_pairs={{0,1},{1,0},{2,3},{3,2},{4,5},{5,4},{6,7},{7,6},{8,9},{9,8},{10,11... | collective-permute-start | bytes 786440 | tf_op jit(solution)/shard_map/ppermute | solution.py:10
  91.4 9.2 %collective-permute-start.7 = (f32[256,1,256]{0,2,1:T(8,128)S(1)}, f32[256,1,256]{0,2,1:T(8,128)S(1)}, u32[]{:S(2)}, u32[]{:S(2)}) collective-permute-start(f32[256,1,256]{0,2,1:T(8,128)S(1)} %fusion.65), channel_id=1, source_target_pairs={{0,2},{1,3},{2,0},{3,1},{4,6},{5,7},{6,4},{7,5},{8,10},{9,11},{10,... | collective-permute-start | bytes 786440 | tf_op jit(solution)/shard_map/ppermute | solution.py:10
  93.1 12.2 %collective-permute-start.5 = (f32[256,1,256]{0,2,1:T(8,128)S(1)}, f32[256,1,256]{0,2,1:T(8,128)S(1)}, u32[]{:S(2)}, u32[]{:S(2)}) collective-permute-start(f32[256,1,256]{0,2,1:T(8,128)S(1)} %fusion.64), channel_id=1, source_target_pairs={{0,2},{1,3},{2,0},{3,1},{4,6},{5,7},{6,4},{7,5},{8,10},{9,11},{10,... | collective-permute-start | bytes 786440 | tf_op jit(solution)/shard_map/ppermute | solution.py:10
where the time goes:
time: 110 us; the launch traced here: 109 us
  matrix products  44.5 us (40%)
  waiting for transfers between devices  34 us (31%)
  starting transfers between devices  16.6 us (15%)
  local copies, waits for them, and re-layouts  8.79 us (8%)
  other arithmetic  4.29 us (4%)
    ppermute x8, waiting for transfers between devices, partner(): lax.ppermute(x, axis, [(i, i ^ 1 << stride) for i in range(lax.axis_size(...  21.1 us
    dot_general x4, matrix products, prepare(): jnp.dot(selector, branch_imag, precision=lax.Precision.HIGHEST, preferred...  10.3 us
    dot_general x4, matrix products, product(): jnp.dot(left_real + left_imag, moved_sum, precision=lax.Precision.HIGHEST...  9.62 us
    all_to_all x1, waiting for transfers between devices, outer_step(): lax.all_to_all(plane_imag, 'outer', split_axis=3, concat_axis=3, tiled=True)  9.42 us
    dot_general x4, matrix products, prepare(): jnp.dot(selector, branch_real, precision=lax.Precision.HIGHEST, preferred...  9.24 us
    dot_general x4, matrix products, product(): jnp.dot(left_real, moved_real, precision=lax.Precision.HIGHEST, preferred...  8.03 us
    dot_general x4, matrix products, product(): jnp.dot(left_imag, moved_imag, precision=lax.Precision.HIGHEST, preferred...  7.39 us
    ppermute x8, starting transfers between devices, partner(): lax.ppermute(x, axis, [(i, i ^ 1 << stride) for i in range(lax.axis_size(...  6.4 us
  transfers between devices with their start and end apart: 10, of which 6 were waited for; matrix products, arithmetic and copies ran while one was open for 27% of the time, Pallas kernels for 0%

commit v1 on v0

v1 whole, which is shorter than its diff:
```python
import functools

import jax
import jax.numpy as jnp
from jax import lax
from jax.experimental import pallas as pl
from jax.experimental.pallas import tpu as pltpu
from jax.sharding import PartitionSpec as P

MESH = pl.DeviceIdType.MESH
LANES = 128
CHUNKS = 4
F32 = jnp.float32
BF16 = jnp.bfloat16


def prepare(branch_real, branch_imag, order):
    width = branch_real.shape[0]
    places = lax.broadcasted_iota(jnp.int32, (width, width), 0)
    selector = (places == order[None, :]).astype(F32)
    dot = functools.partial(jnp.dot, precision=lax.Precision.HIGHEST, preferred_element_type=F32)
    moved_real = dot(selector, branch_real)
    moved_imag = dot(selector, branch_imag)
    return (moved_real, moved_imag, moved_real + moved_imag)


def product(plane_real, plane_imag, prepared):
    moved_real, moved_imag, moved_sum = prepared
    width = moved_real.shape[0]
    count = plane_real.size // width
    dot = functools.partial(jnp.dot, precision=lax.Precision.HIGHEST, preferred_element_type=F32)
    left_real = plane_real.reshape(count, width)
    left_imag = plane_imag.reshape(count, width)
    first = dot(left_real, moved_real)
    second = dot(left_imag, moved_imag)
    third = dot(left_real + left_imag, moved_sum)
    return (
        (first - second).reshape(1, 1, count, width),
        (third - first - second).reshape(1, 1, count, width),
    )


def general(stem_real, stem_imag, branch_real, branch_imag, orders):
    planes = (stem_real, stem_imag)
    swaps = ("inner", "outer", "inner")
    for step in range(branch_real.shape[0]):
        if step:
            planes = [
                lax.all_to_all(x, swaps[step - 1], split_axis=3, concat_axis=3, tiled=True)
                for x in planes
            ]
        planes = product(*planes, prepare(branch_real[step], branch_imag[step], orders[step]))
    return tuple(planes)


def split(x):
    high = x.astype(BF16)
    low = (x - high.astype(F32)).astype(BF16)
    return high, low


def lay_columns(first, second, groups):
    width = first.shape[1]
    share = width // groups
    if share % LANES == 0:
        parts = []
        for g in range(groups):
            parts.append(first[:, g * share : (g + 1) * share])
            parts.append(second[:, g * share : (g + 1) * share])
        return jnp.concatenate(parts, axis=1)
    lower = lax.broadcasted_iota(jnp.int32, (first.shape[0], LANES), 1) < share
    parts = []
    for t in range(width // LANES):
        a = first[:, t * LANES : (t + 1) * LANES]
        b = second[:, t * LANES : (t + 1) * LANES]
        parts.append(jnp.where(lower, a, pltpu.roll(b, share, 1)))
        parts.append(jnp.where(lower, pltpu.roll(a, share, 1), b))
    return jnp.concatenate(parts, axis=1)


def build(order_ref, real_ref, imag_ref, high_ref, low_ref, step, groups_in, groups_out):
    width = real_ref.shape[1]
    share = width // groups_in
    order = order_ref[step : step + 1, :]
    block = min(256, width)
    real_terms = split(real_ref[step])
    imag_terms = split(imag_ref[step])
    for start in range(0, width, block):
        places = lax.broadcasted_iota(jnp.int32, (block, width), 0) + start
        selector = jnp.where(places == order, 1.0, 0.0).astype(BF16)
        for term, out_ref in enumerate((high_ref, low_ref)):
            moved_real = jnp.dot(selector, real_terms[term], preferred_element_type=F32)
            moved_imag = jnp.dot(selector, imag_terms[term], preferred_element_type=F32)
            top = lay_columns(moved_real, moved_imag, groups_out).astype(BF16)
            bottom = lay_columns(-moved_imag, moved_real, groups_out).astype(BF16)
            run = min(share, block)
            for at in range(start, start + block, run):
                group, place = divmod(at, share)
                row = group * 2 * share + place
                part = slice(at - start, at - start + run)
                out_ref[row : row + run, :] = top[part]
                out_ref[row + share : row + share + run, :] = bottom[part]


def kernel(
    axes,
    sizes,
    order_ref,
    stem_real,
    stem_imag,
    branch_real,
    branch_imag,
    out_real,
    out_imag,
    stem,
    real,
    imag,
    highs,
    lows,
    sent0,
    sent1,
    sent2,
    got0,
    got1,
    got2,
    load_sem,
    branch_sem,
    send0,
    send1,
    send2,
    recv0,
    recv1,
    recv2,
):
    products = branch_real.shape[0]
    sent, got = (sent0, sent1, sent2), (got0, got1, got2)
    send_sems, recv_sems = (send0, send1, send2), (recv0, recv1, recv2)
    rows, width = stem_real.shape
    part = rows // CHUNKS
    me = [lax.axis_index(a) for a in axes]

    loads = [
        pltpu.make_async_copy(stem_real, stem.at[0], load_sem.at[0]),
        pltpu.make_async_copy(stem_imag, stem.at[1], load_sem.at[1]),
    ]
    fetches = [
        (
            pltpu.make_async_copy(branch_real.at[p], real.at[p], branch_sem.at[p, 0]),
            pltpu.make_async_copy(branch_imag.at[p], imag.at[p], branch_sem.at[p, 1]),
        )
        for p in range(products)
    ]
    for copy in fetches[0]:
        copy.start()
    for copy in loads:
        copy.start()
    for pair in fetches[1:]:
        for copy in pair:
            copy.start()

    barrier = pltpu.get_barrier_semaphore()
    partners = 0
    for axis in sorted(set(axes)):
        size = sizes[axis]
        mine = lax.axis_index(axis)
        for s in range(1, size):
            pl.semaphore_signal(
                barrier,
                inc=1,
                device_id={axis: lax.rem(mine + s, size)},
                device_id_type=MESH,
            )
            partners += 1

    groups = [1] + [sizes[a] for a in axes] + [1]

    def prep(p):
        for copy in fetches[p]:
            copy.wait()
        build(order_ref, real, imag, highs.at[p], lows.at[p], p, groups[p], groups[p + 1])

    def swap_copy(p, c, s, arriving):
        size = sizes[axes[p]]
        there = lax.rem(me[p] + s, size)
        slot = lax.rem(me[p] + size - s, size) if arriving else me[p]
        return pltpu.make_async_remote_copy(
            src_ref=sent[p].at[there, c],
            dst_ref=got[p].at[slot, c],
            send_sem=send_sems[p].at[c, s - 1],
            recv_sem=recv_sems[p].at[c, s - 1],
            device_id={axes[p]: there},
            device_id_type=MESH,
        )

    def multiply(p, c):
        if p == 0:
            at = pl.ds(pl.multiple_of(c * part, part), part)
            x = jnp.concatenate([stem[0, at, :], stem[1, at, :]], axis=1)
        else:
            for s in range(1, groups[p]):
                swap_copy(p - 1, c, s, True).wait_recv()
            x = jnp.concatenate([got[p - 1][g, c] for g in range(groups[p])], axis=1)
        high, low = split(x)
        both = jnp.concatenate([high, low], axis=0)
        lanes = 2 * width // groups[p + 1]
        block = min(256, 2 * width)
        for start in range(0, 2 * width, block):
            cols = slice(start, start + block)
            y = jnp.dot(both, highs[p, :, cols], preferred_element_type=F32)
            y = y[:part] + y[part:]
            y = y + jnp.dot(high, lows[p, :, cols], preferred_element_type=F32)
            if p == products - 1:
                at = pl.ds(pl.multiple_of(c * part, part), part)
                if start < width:
                    out_real[at, start : start + block] = y
                else:
                    out_imag[at, start - width : start - width + block] = y
            else:
                run = min(block, lanes)
                for k in range(0, block, run):
                    group, place = divmod(start + k, lanes)
                    sent[p][group, c, :, place : place + run] = y[:, k : k + run]
        if p < products - 1:
            if p == 0:
                pass
            for s in range(1, groups[p + 1]):
                swap_copy(p, c, s, False).start()
            got[p][me[p], c] = sent[p][me[p], c]

    def stage(p):
        @pl.loop(0, CHUNKS)
        def _(c):
            multiply(p, c)

    prep(0)
    for copy in loads:
        copy.wait()
    pl.semaphore_wait(barrier, partners)
    stage(0)
    prep(1)
    stage(1)
    for p in range(2, products):
        prep(p)
    stage(2)
    stage(3)

    for p in range(len(axes)):

        @pl.loop(0, CHUNKS)
        def _(c):
            for s in range(1, sizes[axes[p]]):
                swap_copy(p, c, s, False).wait_send()


def fused(sizes, stem_real, stem_imag, branch_real, branch_imag, orders):
    rows, width = stem_real.shape[-2:]
    products = branch_real.shape[0]
    axes = ("inner", "outer", "inner")
    part = rows // CHUNKS

    def buffers():
        return [
            pltpu.VMEM((sizes[a], CHUNKS, part, 2 * width // sizes[a]), F32) for a in axes
        ]

    def semaphores():
        return [pltpu.SemaphoreType.DMA((CHUNKS, sizes[a] - 1)) for a in axes]

    plane = jax.ShapeDtypeStruct((rows, width), F32)
    flops = products * 3 * 2 * rows * (2 * width) ** 2 + products * 8 * width**3
    out_real, out_imag = pl.pallas_call(
        functools.partial(kernel, axes, sizes),
        out_shape=(plane, plane),
        in_specs=[pl.BlockSpec(memory_space=pltpu.VMEM)]
        + [pl.BlockSpec(memory_space=pl.ANY)] * 4,
        out_specs=(pl.BlockSpec(memory_space=pltpu.VMEM),) * 2,
        scratch_shapes=[
            pltpu.VMEM((2, rows, width), F32),
            pltpu.VMEM((products, width, width), F32),
            pltpu.VMEM((products, width, width), F32),
            pltpu.VMEM((products, 2 * width, 2 * width), BF16),
            pltpu.VMEM((products, 2 * width, 2 * width), BF16),
        ]
        + buffers()
        + buffers()
        + [pltpu.SemaphoreType.DMA((2,)), pltpu.SemaphoreType.DMA((products, 2))]
        + semaphores()
        + semaphores(),
        compiler_params=pltpu.CompilerParams(
            collective_id=0, has_side_effects=True, vmem_limit_bytes=56 * 2**20
        ),
        cost_estimate=pl.CostEstimate(
            flops=flops, bytes_accessed=4 * (branch_real.size * 2 + rows * width * 4), transcendentals=0
        ),
    )(
        orders,
        stem_real.reshape(rows, width),
        stem_imag.reshape(rows, width),
        branch_real,
        branch_imag,
    )
    return out_real.reshape(stem_real.shape), out_imag.reshape(stem_imag.shape)


def fits(sizes, rows, width):
    shares = [width // size for size in sizes.values()]
    return (
        all(share % LANES == 0 or 2 * share == LANES for share in shares)
        and rows % (CHUNKS * 16) == 0
        and width % 256 == 0
    )


def solution(mesh):
    sizes = {axis: mesh.shape[axis] for axis in ("outer", "inner")}

    def on_device(stem_real, stem_imag, branch_real, branch_imag, orders):
        arrays = (stem_real, stem_imag, branch_real, branch_imag, orders)
        if fits(sizes, *stem_real.shape[-2:]):
            return fused(sizes, *arrays)
        return general(*arrays)

    planes = P("outer", "inner", None, None)
    return jax.shard_map(
        on_device,
        mesh=mesh,
        in_specs=(planes, planes, P(), P(), P()),
        out_specs=(planes, planes),
        check_vma=False,
    )
```

time: 110 us -> 49.3 us (0.45)
  Pallas kernels: 0 us -> 44.6 us
  matrix products: 44.5 us -> 0 us
  waiting for transfers between devices: 34 us -> 0 us
  starting transfers between devices: 16.6 us -> 0 us
  local copies, waits for them, and re-layouts: 8.79 us -> 3.74 us
  other arithmetic: 4.29 us -> 0 us
    pallas_call x0 -> x1, Pallas kernels: none -> 44.6 us  [fused(): pl.pallas_call(functools.partial(kernel, axes, sizes), out_shape=(plane,...]
    dot_general x20 -> x0, matrix products: 44.5 us -> none  [the longest x4 10.3 us: prepare(): jnp.dot(selector, branch_imag, precision=lax.Precision.HIGHEST, preferred...]
    ppermute x8 -> x0, waiting for transfers between devices: 21.1 us -> none  [partner(): lax.ppermute(x, axis, [(i, i ^ 1 << stride) for i in range(lax.axis_size(...]
    all_to_all x2 -> x0, waiting for transfers between devices: 12.9 us -> none  [the longest x1 9.42 us: outer_step(): lax.all_to_all(plane_imag, 'outer', split_axis=3, concat_axis=3, tiled=True)]
    all_to_all x2 -> x0, starting transfers between devices: 10.2 us -> none  [the longest x1 6.09 us: outer_step(): lax.all_to_all(plane_imag, 'outer', split_axis=3, concat_axis=3, tiled=True)]
    ppermute x8 -> x0, starting transfers between devices: 6.4 us -> none  [partner(): lax.ppermute(x, axis, [(i, i ^ 1 << stride) for i in range(lax.axis_size(...]
    another operation x5 -> x0, local copies, waits for them, and re-layouts: 2.84 us -> none  [the longest x2 2.74 us: pair_section(): viewed = plane.reshape(rows_n, upper, 2, lower * (width // groups))]
    slice x3 -> x0, local copies, waits for them, and re-layouts: 2.37 us -> none  [the longest x2 1.51 us: pair_section(): half_zero = viewed[:, :, 0]]
  transfers between devices with their start and end apart: 10 -> 0, of which waited for: 6 -> 0; matrix products, arithmetic and copies ran while one was open for 27% -> 0% of each run, Pallas kernels for 0% -> 0%
where the time goes in v1:
time: 49.3 us; the launch traced here: 49 us
  Pallas kernels  44.6 us (90%)
  local copies, waits for them, and re-layouts  3.74 us (8%)
  between operations  0.64 us (1%)
    pallas_call x1, Pallas kernels, fused(): pl.pallas_call(functools.partial(kernel, axes, sizes), out_shape=(plane,...  44.6 us
    unnamed x2, local copies, waits for them, and re-layouts  3.74 us

profile of v1, /device:TPU:0, one launch (start us, length us, event | category | flops | bytes accessed | tf_op | source)
XLA Modules:
  0.0 49.0 jit_solution(9385524934389878665)
XLA Ops:
  0.6 44.6 %shard_map.68 = (f32[256,512]{1,0:T(8,128)}, f32[256,512]{1,0:T(8,128)}) custom-call(s32[4,512]{1,0:T(4,128)} %order_ref.1, f32[256,512]{1,0:T(8,128)} %bitcast.6, f32[256,512]{1,0:T(8,128)} %bitcast.7, f32[4,512,512]{2,1,0:T(8,128)} %branch_real.1, f32[4,512,512]{2,1,0:T(8,128)} %branch_imag.1), custom_call_target="tpu_custom_call" | custom-call | flops 10737418240 | bytes 10485760 | tf_op jit(solution)/shard_map/pallas_call | solution.py:271
  45.3 1.9 %copy.9 = f32[1,1,256,512]{3,2,1,0:T(8,128)} copy(f32[1,1,256,512]{3,2,1,0:T(8,128)} %bitcast.5) | data formatting | bytes 1048576
  47.2 1.9 %copy.10 = f32[1,1,256,512]{3,2,1,0:T(8,128)} copy(f32[1,1,256,512]{3,2,1,0:T(8,128)} %bitcast.4) | data formatting | bytes 1048576

commit v2 on v1

v2 whole, which is shorter than its diff:
```python
import functools

import jax
import jax.numpy as jnp
from jax import lax
from jax.experimental import pallas as pl
from jax.experimental.pallas import tpu as pltpu
from jax.sharding import PartitionSpec as P

MESH = pl.DeviceIdType.MESH
LANES = 128
SHARES = (1, 2, 2, 2, 1)
F32 = jnp.float32
BF16 = jnp.bfloat16


def prepare(branch_real, branch_imag, order):
    width = branch_real.shape[0]
    places = lax.broadcasted_iota(jnp.int32, (width, width), 0)
    selector = (places == order[None, :]).astype(F32)
    dot = functools.partial(jnp.dot, precision=lax.Precision.HIGHEST, preferred_element_type=F32)
    moved_real = dot(selector, branch_real)
    moved_imag = dot(selector, branch_imag)
    return (moved_real, moved_imag, moved_real + moved_imag)


def product(plane_real, plane_imag, prepared):
    moved_real, moved_imag, moved_sum = prepared
    width = moved_real.shape[0]
    count = plane_real.size // width
    dot = functools.partial(jnp.dot, precision=lax.Precision.HIGHEST, preferred_element_type=F32)
    left_real = plane_real.reshape(count, width)
    left_imag = plane_imag.reshape(count, width)
    first = dot(left_real, moved_real)
    second = dot(left_imag, moved_imag)
    third = dot(left_real + left_imag, moved_sum)
    return (
        (first - second).reshape(1, 1, count, width),
        (third - first - second).reshape(1, 1, count, width),
    )


def general(stem_real, stem_imag, branch_real, branch_imag, orders):
    planes = (stem_real, stem_imag)
    swaps = ("inner", "outer", "inner")
    for step in range(branch_real.shape[0]):
        if step:
            planes = [
                lax.all_to_all(x, swaps[step - 1], split_axis=3, concat_axis=3, tiled=True)
                for x in planes
            ]
        planes = product(*planes, prepare(branch_real[step], branch_imag[step], orders[step]))
    return tuple(planes)


def split(x):
    high = x.astype(BF16)
    low = (x - high.astype(F32)).astype(BF16)
    return high, low


def lay_columns(first, second, groups):
    width = first.shape[1]
    share = width // groups
    parts = []
    if share % LANES == 0:
        for g in range(groups):
            parts.append(first[:, g * share : (g + 1) * share])
            parts.append(second[:, g * share : (g + 1) * share])
        return jnp.concatenate(parts, axis=1)
    lower = lax.broadcasted_iota(jnp.int32, (first.shape[0], LANES), 1) < share
    for t in range(width // LANES):
        a = first[:, t * LANES : (t + 1) * LANES]
        b = second[:, t * LANES : (t + 1) * LANES]
        parts.append(jnp.where(lower, a, pltpu.roll(b, share, 1)))
        parts.append(jnp.where(lower, pltpu.roll(a, share, 1), b))
    return jnp.concatenate(parts, axis=1)


def part_planes(blocks):
    lanes = blocks[0].shape[1]
    share = lanes // 2
    if share % LANES == 0:
        return (
            jnp.concatenate([x[:, :share] for x in blocks], axis=1),
            jnp.concatenate([x[:, share:] for x in blocks], axis=1),
        )
    lower = lax.broadcasted_iota(jnp.int32, blocks[0].shape, 1) < share
    real, imag = [], []
    for a, b in zip(blocks[::2], blocks[1::2]):
        real.append(jnp.where(lower, a, pltpu.roll(b, share, 1)))
        imag.append(jnp.where(lower, pltpu.roll(a, share, 1), b))
    return jnp.concatenate(real, axis=1), jnp.concatenate(imag, axis=1)


def build(order_ref, real_ref, imag_ref, high_ref, low_ref, step, groups_out):
    width = real_ref.shape[1]
    order = order_ref[step : step + 1, :]
    block = min(256, width)
    real_terms = split(real_ref[step])
    imag_terms = split(imag_ref[step])
    for start in range(0, width, block):
        places = lax.broadcasted_iota(jnp.int32, (block, width), 0) + start
        selector = jnp.where(places == order, 1.0, 0.0).astype(BF16)
        for term, out_ref in enumerate((high_ref, low_ref)):
            moved_real = jnp.dot(selector, real_terms[term], preferred_element_type=F32)
            moved_imag = jnp.dot(selector, imag_terms[term], preferred_element_type=F32)
            laid = lay_columns(moved_real, moved_imag, groups_out)
            out_ref[start : start + block, :] = laid.astype(BF16)


def kernel(
    axes,
    sizes,
    chunks,
    orders,
    stem_real,
    stem_imag,
    branch_real,
    branch_imag,
    out_real,
    out_imag,
    order_ref,
    stem,
    done,
    real,
    imag,
    highs,
    lows,
    sent0,
    sent1,
    sent2,
    got0,
    got1,
    got2,
    load_sem,
    branch_sem,
    out_sem,
    send0,
    send1,
    send2,
    recv0,
    recv1,
    recv2,
):
    products = branch_real.shape[0]
    sent, got = (sent0, sent1, sent2), (got0, got1, got2)
    send_sems, recv_sems = (send0, send1, send2), (recv0, recv1, recv2)
    rows, width = stem_real.shape
    me = [lax.axis_index(a) for a in axes]
    last = products - 1
    places = []
    for c, size in enumerate(chunks):
        at = sum(chunks[:c])
        places.append(slice(at, at + size))

    loads = [
        pltpu.make_async_copy(orders, order_ref, load_sem.at[2]),
        pltpu.make_async_copy(stem_real, stem.at[0], load_sem.at[0]),
        pltpu.make_async_copy(stem_imag, stem.at[1], load_sem.at[1]),
    ]
    fetches = [
        (
            pltpu.make_async_copy(branch_real.at[p], real.at[p], branch_sem.at[p, 0]),
            pltpu.make_async_copy(branch_imag.at[p], imag.at[p], branch_sem.at[p, 1]),
        )
        for p in range(products)
    ]
    for copy in (loads[0], *fetches[0], *loads[1:]):
        copy.start()
    for pair in fetches[1:]:
        for copy in pair:
            copy.start()

    barrier = pltpu.get_barrier_semaphore()
    partners = 0
    for axis in sorted(set(axes)):
        size = sizes[axis]
        mine = lax.axis_index(axis)
        for s in range(1, size):
            pl.semaphore_signal(
                barrier,
                inc=1,
                device_id={axis: lax.rem(mine + s, size)},
                device_id_type=MESH,
            )
            partners += 1

    groups = [1] + [sizes[a] for a in axes] + [1]

    def prep(p):
        for copy in fetches[p]:
            copy.wait()
        build(order_ref, real, imag, highs.at[p], lows.at[p], p, groups[p + 1])

    def swap_copy(p, c, s, arriving):
        size = sizes[axes[p]]
        there = lax.rem(me[p] + s, size)
        slot = lax.rem(me[p] + size - s, size) if arriving else me[p]
        return pltpu.make_async_remote_copy(
            src_ref=sent[p].at[there, places[c]],
            dst_ref=got[p].at[slot, places[c]],
            send_sem=send_sems[p].at[c, s - 1],
            recv_sem=recv_sems[p].at[c, s - 1],
            device_id={axes[p]: there},
            device_id_type=MESH,
        )

    def out_copies(c):
        return (
            pltpu.make_async_copy(
                done.at[0, places[c]], out_real.at[places[c]], out_sem.at[c, 0]
            ),
            pltpu.make_async_copy(
                done.at[1, places[c]], out_imag.at[places[c]], out_sem.at[c, 1]
            ),
        )

    def multiply(p, c):
        size, at = chunks[c], places[c]
        if p == 0:
            xr, xi = stem[0, at, :], stem[1, at, :]
        else:
            for s in range(1, groups[p]):
                swap_copy(p - 1, c, s, True).wait_recv()
            xr, xi = part_planes([got[p - 1][g, at] for g in range(groups[p])])
        high, low = split(jnp.concatenate([xr, xi], axis=0))
        both = jnp.concatenate([high, low], axis=0)

        def columns(start, stop):
            cols = slice(start, stop)
            y = jnp.dot(both, highs[p, :, cols], preferred_element_type=F32)
            y = y[: 2 * size] + y[2 * size :]
            y = y + jnp.dot(high, lows[p, :, cols], preferred_element_type=F32)
            return y[:size], y[size:]

        share = width // groups[p + 1]
        if share % LANES == 0:
            run = min(share, LANES if p < last else 256)
            for group in range(groups[p + 1]):
                for place in range(0, share, run):
                    base = group * 2 * share + place
                    if run == share:
                        yr, yi = columns(base, base + 2 * share)
                        rr, ri = yr[:, :share], yr[:, share:]
                        ir, ii = yi[:, :share], yi[:, share:]
                    else:
                        rr, ir = columns(base, base + run)
                        ri, ii = columns(base + share, base + share + run)
                    if p == last:
                        done[0, at, place : place + run] = rr - ii
                        done[1, at, place : place + run] = ri + ir
                    else:
                        sent[p][group, at, place : place + run] = rr - ii
                        sent[p][group, at, share + place : share + place + run] = ri + ir
        else:
            lower = lax.broadcasted_iota(jnp.int32, (size, LANES), 1) < share
            for group in range(0, groups[p + 1], 2):
                yr, yi = columns(group * LANES, (group + 2) * LANES)
                for k in range(2):
                    a = yr[:, k * LANES : (k + 1) * LANES]
                    b = pltpu.roll(yi[:, k * LANES : (k + 1) * LANES], share, 1)
                    sent[p][group + k, at, :] = a + jnp.where(lower, -b, b)
        if p == last:
            for copy in out_copies(c):
                copy.start()
        else:
            if p == 0 and c == 0:
                pl.semaphore_wait(barrier, partners)
            for s in range(1, groups[p + 1]):
                swap_copy(p, c, s, False).start()
            got[p][me[p], at] = sent[p][me[p], at]

    count = len(chunks)
    loads[0].wait()
    prep(0)
    for copy in loads[1:]:
        copy.wait()
    for c in range(min(2, count)):
        multiply(0, c)
    prep(1)
    for c in range(count):
        multiply(1, c)
        if c + 2 < count:
            multiply(0, c + 2)
        if c == 0:
            prep(2)
        if c == 1:
            prep(3)
    multiply(2, 0)
    for c in range(1, count):
        multiply(2, c)
        multiply(3, c - 1)
    multiply(3, count - 1)

    for c in range(count):
        for p in range(len(axes)):
            for s in range(1, sizes[axes[p]]):
                swap_copy(p, c, s, False).wait_send()
        for copy in out_copies(c):
            copy.wait()


def deliver(real, imag, out_real, out_imag):
    out_real[...] = real[...]
    out_imag[...] = imag[...]


def fused(sizes, stem_real, stem_imag, branch_real, branch_imag, orders):
    rows, width = stem_real.shape[-2:]
    products = branch_real.shape[0]
    axes = ("inner", "outer", "inner")
    chunks = [rows * n // sum(SHARES) for n in SHARES]
    anywhere = pl.BlockSpec(memory_space=pltpu.HBM)

    buffers = [pltpu.VMEM((sizes[a], rows, 2 * width // sizes[a]), F32) for a in axes]
    semaphores = [pltpu.SemaphoreType.DMA((len(chunks), sizes[a] - 1)) for a in axes]
    plane = jax.ShapeDtypeStruct((rows, width), F32)
    flops = products * 3 * 2 * rows * (2 * width) ** 2 + products * 8 * width**3
    planes = pl.pallas_call(
        functools.partial(kernel, axes, sizes, chunks),
        out_shape=(plane, plane),
        in_specs=[anywhere] * 5,
        out_specs=(anywhere, anywhere),
        scratch_shapes=[
            pltpu.VMEM(orders.shape, orders.dtype),
            pltpu.VMEM((2, rows, width), F32),
            pltpu.VMEM((2, rows, width), F32),
            pltpu.VMEM((products, width, width), F32),
            pltpu.VMEM((products, width, width), F32),
            pltpu.VMEM((products, width, 2 * width), BF16),
            pltpu.VMEM((products, width, 2 * width), BF16),
        ]
        + buffers * 2
        + [
            pltpu.SemaphoreType.DMA((3,)),
            pltpu.SemaphoreType.DMA((products, 2)),
            pltpu.SemaphoreType.DMA((len(chunks), 2)),
        ]
        + semaphores * 2,
        compiler_params=pltpu.CompilerParams(
            collective_id=0, has_side_effects=True, vmem_limit_bytes=56 * 2**20
        ),
        cost_estimate=pl.CostEstimate(
            flops=flops,
            bytes_accessed=4 * (branch_real.size * 2 + rows * width * 4),
            transcendentals=0,
        ),
    )(
        orders,
        stem_real.reshape(rows, width),
        stem_imag.reshape(rows, width),
        branch_real,
        branch_imag,
    )
    whole = pl.BlockSpec(memory_space=pltpu.VMEM)
    planes = pl.pallas_call(
        deliver,
        out_shape=(plane, plane),
        in_specs=[whole, whole],
        out_specs=(whole, whole),
    )(*planes)
    return tuple(x.reshape(stem_real.shape) for x in planes)


def fits(sizes, rows, width):
    shares = [width // size for size in sizes.values()]
    return (
        all(share % LANES == 0 or 2 * share == LANES for share in shares)
        and rows % (sum(SHARES) * 16) == 0
        and width % 256 == 0
    )


def solution(mesh):
    sizes = {axis: mesh.shape[axis] for axis in ("outer", "inner")}

    def on_device(stem_real, stem_imag, branch_real, branch_imag, orders):
        arrays = (stem_real, stem_imag, branch_real, branch_imag, orders)
        if fits(sizes, *stem_real.shape[-2:]):
            return fused(sizes, *arrays)
        return general(*arrays)

    planes = P("outer", "inner", None, None)
    return jax.shard_map(
        on_device,
        mesh=mesh,
        in_specs=(planes, planes, P(), P(), P()),
        out_specs=(planes, planes),
        check_vma=False,
    )
```

time: 49.3 us -> 45 us (0.913)
  local copies, waits for them, and re-layouts: 3.74 us -> 0 us
    unnamed x2 -> x0, local copies, waits for them, and re-layouts: 3.74 us -> none
    pallas_call x1 -> x2, Pallas kernels: 44.6 us -> 44.2 us  [the longest x1 42 us: fused(): pl.pallas_call(functools.partial(kernel, axes, sizes, chunks), out_shape=...]
where the time goes in v2:
time: 45 us; the launch traced here: 44.9 us
  Pallas kernels  44.2 us (98%)
  between operations  0.64 us (1%)
    pallas_call x1, Pallas kernels, fused(): pl.pallas_call(functools.partial(kernel, axes, sizes, chunks), out_shape=...  42 us
    pallas_call x1, Pallas kernels, fused(): pl.pallas_call(deliver, out_shape=(plane, plane), in_specs=[whole, whole]...  2.2 us

profile of v2, /device:TPU:0, one launch (start us, length us, event | category | flops | bytes accessed | tf_op | source)
XLA Modules:
  0.0 44.9 jit_solution(7037705917325352129)
XLA Ops:
  0.6 42.0 %shard_map.68 = (f32[256,512]{1,0:T(8,128)}, f32[256,512]{1,0:T(8,128)}) custom-call(s32[4,512]{1,0:T(4,128)} %orders.1, f32[256,512]{1,0:T(8,128)} %bitcast.4, f32[256,512]{1,0:T(8,128)} %bitcast.5, f32[4,512,512]{2,1,0:T(8,128)} %branch_real.1, f32[4,512,512]{2,1,0:T(8,128)} %branch_imag.1), custom_call_target="tpu_custom_call" | custom-call | flops 10737418240 | bytes 10485760 | tf_op jit(solution)/shard_map/pallas_call | solution.py:320
  42.7 2.2 %shard_map.69 = (f32[256,512]{1,0:T(8,128)}, f32[256,512]{1,0:T(8,128)}) custom-call(f32[256,512]{1,0:T(8,128)} %get-tuple-element.6.real, f32[256,512]{1,0:T(8,128)} %get-tuple-element.7.imag), custom_call_target="tpu_custom_call" | custom-call | tf_op jit(solution)/shard_map/pallas_call | solution.py:357
